TPU v7x, 256 devices: a whole 4x4x8 slice. The times are simulated.
256 devices in a mesh: row: 8 (over x, core), col: 32 (over y, z).
Axes of the slice: x: 4, y: 4, z: 8, core: 2. Of those that a mesh axis runs over, the one named last changes fastest.
Arguments:
- features: bfloat16 [65536, 256], P(('row', 'col')), may hold values from -6 to 6
- neighbours: int32 [10, 65536], P(None, ('row', 'col')), may hold values from 0 to 511, as said below
- halo_ids: int32 [256, 1, 256], P(('row', 'col')), may hold values from 0 to 255
- w_self: bfloat16 [256, 256], replicated, may hold values from -0.375 to 0.375
- w_neigh: bfloat16 [256, 256], replicated, may hold values from -0.75 to 0.75
- b_sage: float32 [256], replicated, may hold values from -3 to 3
- w_first: bfloat16 [512, 256], replicated, may hold values from -0.25 to 0.25
- b_first: float32 [256], replicated, may hold values from -3 to 3
- w_second: bfloat16 [256], replicated, may hold values from -1.5 to 1.5
- b_second: float32 [1], replicated, may hold values from -3 to 3
- src_owner: int32 [8, 32, 8192, 1], P('row', 'col'), may hold values from 0 to 31; in each aligned block of 8192 rows (0 to 8191, 8192 to 16383, ..., all dimensions but the last counted through in order) at most 320 rows name the same one
- src_local: int32 [8, 32, 8192], P('row', 'col'), may hold values from 0 to 255
- dst_index: int32 [8, 32, 8192], P('row', 'col'), may hold values from 0 to 2047
- labels: int32 [8, 32, 8192], P('row', 'col'), may hold values 0 or 1
Outputs:
- embeds: bfloat16 [65536, 256], P(('row', 'col'))
- logits: float32 [8, 32, 8192], P('row', 'col')
- node_grad: float32 [65536, 256], P(('row', 'col'))
- grad_self: float32 [256, 256], replicated
- grad_neigh: float32 [256, 256], replicated
- grad_bsage: float32 [256], replicated
- grad_first: float32 [32, 512, 256], P('col')
- grad_bfirst: float32 [32, 256], P('col')
- grad_second: float32 [32, 256], P('col')
Inputs may be any that keep to these rules, and one draw needn't show every extreme that they name: `neighbours`: in each partition every one of the 256 received rows (values 256 and up) is named by exactly one entry; the other entries name the partition's own rows. `src_owner`: among the 8192 edges of one tile at most 320 name the same source partition, and that many are reached.
All inputs are finite; a program needn't handle non-finite values. No bound on the sum of `labels` on one device may be relied on, other than what follows from the above.
Results may differ from a plain program's by a relative error of at most 0.0052.
Values may be sent and summed in bfloat16 or wider, within the bound.
No kernel may reach another device: no remote copies, remote signals or barrier semaphores. Data moves between devices by JAX's collectives and lax.ppermute only.
A program may use at most 128 MiB of HBM per device.

v0:
```python
import jax
import jax.numpy as jnp
from jax import lax
from jax.sharding import PartitionSpec as P


def per_device(
    features,
    neighbours,
    halo_ids,
    w_self,
    w_neigh,
    b_sage,
    w_first,
    b_first,
    w_second,
    b_second,
    src_owner,
    src_local,
    dst_index,
    labels,
):
    node_dev, feat_width = features.shape
    fanout = neighbours.shape[0]
    row_count = lax.axis_size("row")
    col_count = lax.axis_size("col")
    outgoing = features[halo_ids[0]]
    halo_count = outgoing.shape[0]
    outgoing = outgoing.reshape(halo_count, row_count, col_count, feat_width)
    received = lax.all_to_all(
        lax.all_to_all(outgoing, "row", split_axis=1, concat_axis=1, tiled=True),
        "col",
        split_axis=2,
        concat_axis=2,
        tiled=True,
    )
    extended = jnp.concatenate([features, received.reshape(-1, feat_width)], axis=0)
    gathered = extended[neighbours].astype(jnp.float32)
    aggregate = (jnp.sum(gathered, axis=0) / fanout).astype(jnp.bfloat16)
    embed_f = jnp.dot(features, w_self, preferred_element_type=jnp.float32)
    embed_f = embed_f + jnp.dot(aggregate, w_neigh, preferred_element_type=jnp.float32) + b_sage
    embeds = embed_f.astype(jnp.bfloat16)
    owners = src_owner[0, 0, :, 0]
    local_rows = src_local[0, 0]
    dest_rows = dst_index[0, 0]
    targets = labels[0, 0].astype(jnp.float32)
    edge_count = owners.shape[0]
    src_block = lax.all_gather(embeds, "col", axis=0, tiled=True)
    block_rows = owners * node_dev + local_rows
    src_embed = src_block[block_rows]
    dst_block = lax.all_gather(embeds, "row", axis=0, tiled=True)
    dst_embed = dst_block[dest_rows]
    w_src = w_first[:feat_width]
    w_dst = w_first[feat_width:]
    preact = jnp.dot(src_embed, w_src, preferred_element_type=jnp.float32)
    preact = preact + jnp.dot(dst_embed, w_dst, preferred_element_type=jnp.float32) + b_first
    gate_sig = jax.nn.sigmoid(preact)
    hidden = preact * gate_sig
    hidden_b = hidden.astype(jnp.bfloat16)
    logits = jnp.dot(hidden_b, w_second, preferred_element_type=jnp.float32) + b_second[0]
    dlogit = jax.nn.sigmoid(logits) - targets
    second_f = w_second.astype(jnp.float32)
    dpreact = dlogit[:, None] * second_f[None, :] * gate_sig * (1.0 + preact * (1.0 - gate_sig))
    dpreact_b = dpreact.astype(jnp.bfloat16)
    part_second = jnp.sum(hidden * dlogit[:, None], axis=0)
    part_bfirst = jnp.sum(dpreact, axis=0)
    grad_src = jnp.dot(src_embed.T, dpreact_b, preferred_element_type=jnp.float32)
    grad_dst = jnp.dot(dst_embed.T, dpreact_b, preferred_element_type=jnp.float32)
    part_first = jnp.concatenate([grad_src, grad_dst], axis=0)
    decoder_sums = lax.psum((part_first, part_bfirst, part_second), "row")
    src_rows_g = jnp.dot(dpreact_b, w_src.T, preferred_element_type=jnp.float32).astype(
        jnp.bfloat16
    )
    dst_rows_g = jnp.dot(dpreact_b, w_dst.T, preferred_element_type=jnp.float32).astype(
        jnp.bfloat16
    )
    src_acc = (
        jnp.zeros((src_block.shape[0], feat_width), jnp.float32)
        .at[block_rows]
        .add(src_rows_g.astype(jnp.float32))
    )
    src_grad = lax.psum_scatter(src_acc, "col", scatter_dimension=0, tiled=True)
    dest_acc = (
        jnp.zeros((dst_block.shape[0], feat_width), jnp.float32)
        .at[dest_rows]
        .add(dst_rows_g.astype(jnp.float32))
    )
    dest_grad = lax.psum_scatter(dest_acc, "row", scatter_dimension=0, tiled=True)
    node_grad = src_grad + dest_grad
    node_grad_b = node_grad.astype(jnp.bfloat16)
    part_self = jnp.dot(features.T, node_grad_b, preferred_element_type=jnp.float32)
    part_neigh = jnp.dot(aggregate.T, node_grad_b, preferred_element_type=jnp.float32)
    part_bsage = jnp.sum(node_grad, axis=0)
    encoder_sums = lax.psum((part_self, part_neigh, part_bsage), ("row", "col"))
    return (
        embeds,
        logits.reshape(1, 1, edge_count),
        node_grad,
        encoder_sums[0],
        encoder_sums[1],
        encoder_sums[2],
        decoder_sums[0][None],
        decoder_sums[1][None],
        decoder_sums[2][None],
    )


def solution(mesh):
    placed = (
        P(("row", "col"), None),
        P(None, ("row", "col")),
        P(("row", "col"), None, None),
        P(),
        P(),
        P(),
        P(),
        P(),
        P(),
        P(),
        P("row", "col", None, None),
        P("row", "col", None),
        P("row", "col", None),
        P("row", "col", None),
    )
    return jax.shard_map(
        per_device,
        mesh=mesh,
        in_specs=placed,
        out_specs=(
            P(("row", "col"), None),
            P("row", "col", None),
            P(("row", "col"), None),
            P(),
            P(),
            P(),
            P("col", None, None),
            P("col", None),
            P("col", None),
        ),
        check_vma=False,
    )
```

profile of v0, /device:TPU:8, one launch (start us, length us, event | category | flops | bytes accessed | tf_op | source)
XLA Modules:
  0.0 875.0 jit_solution(14454785513505962907)
XLA Ops:
  7.2 0.0 copy-start
  7.2 0.0 copy-start.13
  7.2 0.0 copy-start.7
  7.2 0.7 compare_select_fusion.3
  8.0 2.5 gather_fusion
  10.5 0.0 copy-start.11
  10.5 4.4 all-to-all-start
  15.0 0.7 compare_select_fusion.2
  15.7 5.4 all-to-all-done
  21.1 0.7 copy.26
  21.8 11.7 %all-to-all-start.1 = ((bf16[1,8,32,256]{3,1,0,2:T(8,128)(2,1)}), bf16[1,8,32,256]{3,1,0,2:T(8,128)(2,1)S(1)}, u32[]{:S(2)}, u32[]{:S(2)}) async-start(bf16[1,8,32,256]{3,1,0,2:T(8,128)(2,1)} %copy.26), calls=%async_computation.1 | async-start | bytes 262144 | tf_op jit(solution)/shard_map/all_to_all | solution.py:30
  33.6 0.0 all-gather.5.cloned.1.call-start
  33.6 1.1 fusion.26
  34.7 7.9 all-to-all-done.1
  42.7 0.9 pad_maximum_fusion
  43.6 7.6 gather_fusion.1
  51.2 0.2 convert_reduce_fusion
  51.4 0.9 fusion.10
  52.2 0.0 all-gather.5.cloned.1.call-update
  52.3 0.0 all-gather.3.cloned.1.call-start
  52.3 0.7 all-gather.3.cloned.1.call-update
  53.0 0.2 reduce-scatter.5.cloned.1.call-start
  53.2 0.0 copy-done.14
  53.9 0.0 copy-done.10
  54.0 0.1 compare_select_fusion.1
  54.1 18.4 %all-gather.5.cloned.1.call-done = bf16[2048,256]{1,0:T(8,128)(2,1)} async-done(((bf16[256,256]{1,0:T(8,128)(2,1)}), bf16[2048,256]{1,0:T(8,128)(2,1)}) %all-gather.5.cloned.1.call-update) | async-done | bytes 1048592 | tf_op jit(solution)/shard_map/all_gather | solution.py:51
  72.6 32.2 %gather_fusion.3 = bf16[8192,256]{1,0:T(8,128)(2,1)} fusion(bf16[2048,256]{1,0:T(8,128)(2,1)} %all-gather.5.cloned.1.call-done, s32[8192]{0:T(1024)S(1)} %broadcast_clamp_fusion), kind=kCustom, calls=%fused_computation.3 | custom fusion | bytes 8421376 | tf_op jit(solution)/shard_map/gather | solution.py:52
  104.8 51.4 %all-gather.3.cloned.1.call-done = bf16[8192,256]{1,0:T(8,128)(2,1)} async-done(((bf16[256,256]{1,0:T(8,128)(2,1)}), bf16[8192,256]{1,0:T(8,128)(2,1)}) %all-gather.3.cloned.1.call-update) | async-done | bytes 4194320 | tf_op jit(solution)/shard_map/all_gather | solution.py:48
  156.2 33.6 %gather_fusion.2 = bf16[8192,256]{1,0:T(8,128)(2,1)} fusion(bf16[8192,256]{1,0:T(8,128)(2,1)} %all-gather.3.cloned.1.call-done, s32[8192]{0:T(1024)S(1)} %broadcast_clamp_fusion.1), kind=kCustom, calls=%fused_computation.2 | custom fusion | bytes 8421376 | tf_op jit(solution)/shard_map/gather | solution.py:50
  189.8 0.0 copy-done.6
  189.8 3.6 fusion.16
  193.4 1.3 fusion
  194.7 2.4 fusion.6
  197.1 0.6 divide_subtract_fusion
  197.8 5.9 fusion.24
  203.6 2.0 copy-done.2
  205.6 4.5 fusion.1
  210.1 46.0 %scatter_custom_fusion.1 = f32[2048,256]{1,0:T(8,128)} fusion(s32[8192]{0:T(1024)S(1)} %bitcast.48, f32[8192,256]{1,0:T(8,128)} %fusion.1, f32[]{:T(128)} %constant.11.clone.1), kind=kCustom, calls=%fused_computation.25 | custom fusion | flops 2097152 | bytes 2097664 | tf_op jit(solution)/shard_map/scatter-add | solution.py:86
  256.1 0.0 reduce-scatter.5.cloned.1.call-update
  256.2 0.3 reduce-scatter.3.cloned.1.call-start
  256.4 6.7 fusion.2
  263.1 48.3 %scatter_custom_fusion = f32[8192,256]{1,0:T(8,128)} fusion(s32[8192]{0:T(1024)S(1)} %bitcast.46, f32[8192,256]{1,0:T(8,128)} %fusion.2, f32[]{:T(128)} %constant.11.clone.1), kind=kCustom, calls=%fused_computation.16 | custom fusion | flops 2097152 | bytes 8389120 | tf_op jit(solution)/shard_map/scatter-add | solution.py:80
  311.5 0.0 reduce-scatter.3.cloned.1.call-update
  311.5 0.0 copy-start.4
  311.5 0.0 all-reduce.7.cloned.1.call-start
  311.5 4.8 fusion.27
  316.3 0.0 reduce-scatter.5.cloned.1.call-done
  316.3 221.9 %reduce-scatter.3.cloned.1.call-done = f32[256,256]{1,0:T(8,128)} async-done(((f32[8192,256]{1,0:T(8,128)}), f32[256,256]{1,0:T(8,128)}) %reduce-scatter.3.cloned.1.call-update) | async-done | bytes 262160 | tf_op jit(solution)/shard_map/reduce_scatter | solution.py:82
  538.3 1.1 fusion.25
  539.4 0.9 fusion.18
  540.3 0.9 convolution_bitcast_fusion
  541.3 0.0 all-reduce.7.cloned.1.call-update
  541.3 0.0 copy-start.1
  541.3 0.0 all-reduce.5.cloned.1.call-start
  541.3 4.8 fusion.28
  546.1 0.8 maximum_bitcast_fusion
  547.0 0.0 all-reduce.5.cloned.1.call-update
  547.0 13.0 %all-reduce.1 = (f32[1,256]{1,0:T(1,128)}, f32[1,256]{1,0:T(1,128)}) all-reduce(f32[1,256]{1,0:T(1,128)S(1)} %bitcast.52, f32[1,256]{1,0:T(1,128)S(1)} %bitcast.53), channel_id=1, replica_groups=mesh['row'=8,'col'=32] {'row'}, use_global_device_ids=true, to_apply=%region_11.0 | all-reduce | flops 512 | bytes 4096 | tf_op jit(solution)/shard_map/psum | solution.py:70
  560.0 74.7 %psum.44 = f32[256]{0:T(256)} all-reduce(f32[256]{0:T(256)S(1)} %get-tuple-element.42), channel_id=1, replica_groups=mesh['row'=8,'col'=32] {'row','col'}, use_global_device_ids=true, to_apply=%region_8.0 | all-reduce | flops 256 | bytes 2048 | tf_op jit(solution)/shard_map/psum | solution.py:94
  634.6 162.6 %all-reduce.7.cloned.1.call-done = (f32[256,256]{0,1:T(8,128)}, f32[256,256]{1,0:T(8,128)}) async-done(((f32[256,256]{0,1:T(8,128)}, f32[256,256]{1,0:T(8,128)}), (f32[256,256]{0,1:T(8,128)}, f32[256,256]{1,0:T(8,128)})) %all-reduce.7.cloned.1.call-update) | async-done | bytes 524304 | tf_op jit(solution)/shard_map/psum | solution.py:94
  797.2 1.8 copy.28
  799.0 65.6 %all-reduce.5.cloned.1.call-done = f32[1,512,256]{2,1,0:T(8,128)} async-done(((f32[1,512,256]{2,1,0:T(8,128)}), f32[1,512,256]{2,1,0:T(8,128)}) %all-reduce.5.cloned.1.call-update) | async-done | bytes 524304 | tf_op jit(solution)/shard_map/psum | solution.py:70
  864.6 1.7 copy.33
  866.2 1.9 copy.34
  (30 shorter events, 0.2 us)
Async XLA Ops:
  7.2 26.4 %copy-start = (bf16[256,256]{1,0:T(8,128)(2,1)S(1)}, bf16[256,256]{1,0:T(8,128)(2,1)}, u32[]{:S(2)}) copy-start(bf16[256,256]{1,0:T(8,128)(2,1)} %param.17) | copy-start | bytes 393220
  7.2 44.2 %copy-start.13 = (f32[256]{0:T(256)S(1)}, f32[256]{0:T(256)}, u32[]{:S(2)}) copy-start(f32[256]{0:T(256)} %param.19) | copy-start | bytes 3076
  7.2 44.2 %copy-start.7 = (bf16[256,256]{1,0:T(8,128)(2,1)S(1)}, bf16[256,256]{1,0:T(8,128)(2,1)}, u32[]{:S(2)}) copy-start(bf16[256,256]{1,0:T(8,128)(2,1)} %param.18) | copy-start | bytes 393220
  10.5 42.7 %copy-start.14 = (bf16[256]{0:T(256)(128)(2,1)S(1)}, bf16[256]{0:T(256)(128)(2,1)}, u32[]{:S(2)}) copy-start(bf16[256]{0:T(256)(128)(2,1)} %param.22) | copy-start | bytes 1540
  10.5 43.4 %copy-start.10 = (s32[1,1,8192]{2,1,0:T(1,128)S(1)}, s32[1,1,8192]{2,1,0:T(1,128)}, u32[]{:S(2)}) copy-start(s32[1,1,8192]{2,1,0:T(1,128)} %param.27) | copy-start | bytes 98308
  10.5 43.4 %copy-start.8 = (s32[1,1,8192]{2,1,0:T(1,128)S(1)}, s32[1,1,8192]{2,1,0:T(1,128)}, u32[]{:S(2)}) copy-start(s32[1,1,8192]{2,1,0:T(1,128)} %param.25) | copy-start | bytes 98308
  10.5 43.5 %copy-start.9 = (s32[1,1,8192,1]{2,3,1,0:T(1,128)S(1)}, s32[1,1,8192,1]{2,3,1,0:T(1,128)}, u32[]{:S(2)}) copy-start(s32[1,1,8192,1]{2,3,1,0:T(1,128)} %param.24) | copy-start | bytes 98308
  10.5 43.5 %copy-start.11 = (s32[1,1,8192]{2,1,0:T(1,128)S(1)}, s32[1,1,8192]{2,1,0:T(1,128)}, u32[]{:S(2)}) copy-start(s32[1,1,8192]{2,1,0:T(1,128)} %param.26) | copy-start | bytes 98308
  10.5 10.6 %all-to-all-start = ((bf16[1,8,32,256]{3,2,0,1:T(8,128)(2,1)}), bf16[1,8,32,256]{3,2,0,1:T(8,128)(2,1)S(1)}, u32[]{:S(2)}, u32[]{:S(2)}) async-start(bf16[1,8,32,256]{3,2,0,1:T(8,128)(2,1)} %bitcast.3), calls=%async_computation | async-start | bytes 262144 | tf_op jit(solution)/shard_map/all_to_all | solution.py:31
  21.8 20.8 %all-to-all-start.1 = ((bf16[1,8,32,256]{3,1,0,2:T(8,128)(2,1)}), bf16[1,8,32,256]{3,1,0,2:T(8,128)(2,1)S(1)}, u32[]{:S(2)}, u32[]{:S(2)}) async-start(bf16[1,8,32,256]{3,1,0,2:T(8,128)(2,1)} %copy.26), calls=%async_computation.1 | async-start | bytes 262144 | tf_op jit(solution)/shard_map/all_to_all | solution.py:30
  33.6 39.0 %all-gather.5.cloned.1.call-start = ((), (), s32[]{:S(2)}) async-start(), calls=%async_computation.5 | async-start | bytes 1179648 | tf_op jit(solution)/shard_map/all_gather | solution.py:51
  52.3 103.9 %all-gather.3.cloned.1.call-start = ((), (), s32[]{:S(2)}) async-start(), calls=%async_computation.4 | async-start | bytes 4325376 | tf_op jit(solution)/shard_map/all_gather | solution.py:48
  53.0 263.3 %reduce-scatter.5.cloned.1.call-start = ((), (), s32[]{:S(2)}) async-start(), calls=%async_computation.7 | async-start | bytes 2359296 | tf_op jit(solution)/shard_map/reduce_scatter | solution.py:88
  104.8 85.0 %copy-start.6 = (bf16[512,256]{1,0:T(8,128)(2,1)S(1)}, bf16[512,256]{1,0:T(8,128)(2,1)}, u32[]{:S(2)}) copy-start(bf16[512,256]{1,0:T(8,128)(2,1)} %param.20) | copy-start | bytes 786436
  189.8 3.6 copy-start.3
  189.8 3.6 copy-start.12
  203.6 2.0 copy-start.2
  256.2 282.1 %reduce-scatter.3.cloned.1.call-start = ((), (), s32[]{:S(2)}) async-start(), calls=%async_computation.6 | async-start | bytes 8650752 | tf_op jit(solution)/shard_map/reduce_scatter | solution.py:82
  311.5 228.8 %copy-start.4 = (bf16[256,256]{1,0:T(8,128)(2,1)S(1)}, bf16[256,256]{1,0:T(8,128)(2,1)}, u32[]{:S(2)}) copy-start(bf16[256,256]{1,0:T(8,128)(2,1)} %param.14) | copy-start | bytes 393220
  311.5 485.7 %all-reduce.7.cloned.1.call-start = ((), (), s32[]{:S(2)}) async-start(), calls=%async_computation.9 | async-start | bytes 1048576 | tf_op jit(solution)/shard_map/psum | solution.py:94
  539.4 6.7 copy-start.5
  541.3 326.8 %copy-start.1 = (bf16[256,256]{1,0:T(8,128)(2,1)S(1)}, bf16[256,256]{1,0:T(8,128)(2,1)}, u32[]{:S(2)}) copy-start(bf16[256,256]{1,0:T(8,128)(2,1)} %param.17) | copy-start | bytes 393220
  541.3 323.3 %all-reduce.5.cloned.1.call-start = ((), (), s32[]{:S(2)}) async-start(), calls=%async_computation.8 | async-start | bytes 1048576 | tf_op jit(solution)/shard_map/psum | solution.py:70
Sparse Core Ops, SparseCore 0:
  52.4 20.1 all-gather.4
  75.7 80.4 all-gather.2
  256.3 34.6 reduce-scatter.4
  311.6 226.6 reduce-scatter.2
  545.3 251.9 all-reduce.6
  800.1 64.4 all-reduce.4
where the time goes:
time: 876 us; the launch traced here: 875 us
  waiting for transfers between devices  534 us (61%)
  other arithmetic  105 us (12%)
  blocking collectives  87.7 us (10%)
  local copies, waits for them, and re-layouts  84.1 us (10%)
  matrix products  31.8 us (4%)
  starting transfers between devices  16.8 us (2%)
  between operations  15.1 us (2%)
    reduce_scatter x1, waiting for transfers between devices, per_device(): src_grad = lax.psum_scatter(src_acc, 'col', scatter_dimension=0, tiled=True)  222 us
    psum x1, waiting for transfers between devices, per_device(): encoder_sums = lax.psum((part_self, part_neigh, part_bsage), ('row', 'col'))  163 us
    psum x1, blocking collectives, per_device(): encoder_sums = lax.psum((part_self, part_neigh, part_bsage), ('row', 'col'))  74.7 us
    psum x1, waiting for transfers between devices, per_device(): decoder_sums = lax.psum((part_first, part_bfirst, part_second), 'row')  65.6 us
    all_gather x1, waiting for transfers between devices, per_device(): src_block = lax.all_gather(embeds, 'col', axis=0, tiled=True)  51.4 us
    scatter-add x1, other arithmetic, per_device(): src_acc = jnp.zeros((src_block.shape[0], feat_width), jnp.float32).at[blo...  48.3 us
    scatter-add x1, other arithmetic, per_device(): dest_acc = jnp.zeros((dst_block.shape[0], feat_width), jnp.float32).at[de...  46 us
    gather x1, local copies, waits for them, and re-layouts, per_device(): src_embed = src_block[block_rows]  33.6 us
  transfers between devices with their start and end apart: 8, of which 7 were waited for; matrix products, arithmetic and copies ran while one was open for 12% of the time, Pallas kernels for 0%

commit v1 on v0

--- a/solution.py
+++ b/solution.py
@@ -91,7 +91,7 @@
     part_self = jnp.dot(features.T, node_grad_b, preferred_element_type=jnp.float32)
     part_neigh = jnp.dot(aggregate.T, node_grad_b, preferred_element_type=jnp.float32)
     part_bsage = jnp.sum(node_grad, axis=0)
-    encoder_sums = lax.psum((part_self, part_neigh, part_bsage), ("row", "col"))
+    encoder_sums = lax.psum(lax.psum((part_self, part_neigh, part_bsage), "col"), "row")
     return (
         embeds,
         logits.reshape(1, 1, edge_count),

time: 876 us -> 789 us (0.901); the launches traced: 875 us -> 776 us
  waiting for transfers between devices: 534 us -> 447 us
  blocking collectives: 87.7 us -> 75.8 us
    psum x2, waiting for transfers between devices: 228 us -> 141 us  [the longest x1 141 us: per_device(): lax.psum((part_self, part_neigh, part_bsage), 'col')]
    psum x2, blocking collectives: 87.7 us -> 75.8 us  [the longest x1 62.9 us: per_device(): lax.psum((part_self, part_neigh, part_bsage), 'col')]
  transfers between devices with their start and end apart: 8 -> 8, of which waited for: 7 -> 6; matrix products, arithmetic and copies ran while one was open for 12% -> 13% of each run, Pallas kernels for 0% -> 0%
where the time goes in v1:
time: 789 us; the launch traced here: 776 us
  waiting for transfers between devices  447 us (57%)
  other arithmetic  105 us (13%)
  local copies, waits for them, and re-layouts  84.2 us (11%)
  blocking collectives  75.8 us (10%)
  matrix products  31.8 us (4%)
  starting transfers between devices  16.8 us (2%)
  between operations  15.1 us (2%)
    reduce_scatter x1, waiting for transfers between devices, per_device(): src_grad = lax.psum_scatter(src_acc, 'col', scatter_dimension=0, tiled=True)  222 us
    psum x1, waiting for transfers between devices, per_device(): lax.psum((part_self, part_neigh, part_bsage), 'col')  141 us
    psum x1, blocking collectives, per_device(): lax.psum((part_self, part_neigh, part_bsage), 'col')  62.9 us
    all_gather x1, waiting for transfers between devices, per_device(): src_block = lax.all_gather(embeds, 'col', axis=0, tiled=True)  51.3 us
    scatter-add x1, other arithmetic, per_device(): src_acc = jnp.zeros((src_block.shape[0], feat_width), jnp.float32).at[blo...  48.3 us
    scatter-add x1, other arithmetic, per_device(): dest_acc = jnp.zeros((dst_block.shape[0], feat_width), jnp.float32).at[de...  46 us
    gather x1, local copies, waits for them, and re-layouts, per_device(): src_embed = src_block[block_rows]  33.7 us
    gather x1, local copies, waits for them, and re-layouts, per_device(): dst_embed = dst_block[dest_rows]  32.3 us
  transfers between devices with their start and end apart: 8, of which 6 were waited for; matrix products, arithmetic and copies ran while one was open for 13% of the time, Pallas kernels for 0%

profile of v1, /device:TPU:8, one launch (start us, length us, event | category | flops | bytes accessed | tf_op | source)
XLA Modules:
  0.0 776.3 jit_solution(7574049874547176835)
XLA Ops:
  7.2 0.0 copy-start
  7.2 0.0 copy-start.13
  7.2 0.0 copy-start.7
  7.2 0.7 compare_select_fusion.3
  8.0 2.5 gather_fusion
  10.5 0.0 copy-start.11
  10.5 4.4 all-to-all-start
  15.0 0.7 compare_select_fusion.2
  15.7 5.4 all-to-all-done
  21.1 0.7 copy.26
  21.8 11.7 %all-to-all-start.1 = ((bf16[1,8,32,256]{3,1,0,2:T(8,128)(2,1)}), bf16[1,8,32,256]{3,1,0,2:T(8,128)(2,1)S(1)}, u32[]{:S(2)}, u32[]{:S(2)}) async-start(bf16[1,8,32,256]{3,1,0,2:T(8,128)(2,1)} %copy.26), calls=%async_computation.1 | async-start | bytes 262144 | tf_op jit(solution)/shard_map/all_to_all | solution.py:30
  33.6 0.0 all-gather.5.cloned.1.call-start
  33.6 0.0 copy-done
  33.6 1.1 fusion.26
  34.7 7.9 %all-to-all-done.1 = bf16[1,8,32,256]{3,1,0,2:T(8,128)(2,1)S(1)} async-done(((bf16[1,8,32,256]{3,1,0,2:T(8,128)(2,1)}), bf16[1,8,32,256]{3,1,0,2:T(8,128)(2,1)S(1)}, u32[]{:S(2)}, u32[]{:S(2)}) %all-to-all-start.1) | async-done | bytes 131104 | tf_op jit(solution)/shard_map/all_to_all | solution.py:30
  42.7 0.9 pad_maximum_fusion
  43.6 7.6 gather_fusion.1
  51.2 0.2 convert_reduce_fusion
  51.4 0.9 fusion.10
  52.2 0.0 all-gather.5.cloned.1.call-update
  52.3 0.0 all-gather.3.cloned.1.call-start
  52.3 0.7 all-gather.3.cloned.1.call-update
  53.0 0.2 reduce-scatter.5.cloned.1.call-start
  53.2 0.0 copy-done.14
  53.9 0.0 copy-done.10
  54.0 0.1 compare_select_fusion.1
  54.1 18.4 %all-gather.5.cloned.1.call-done = bf16[2048,256]{1,0:T(8,128)(2,1)} async-done(((bf16[256,256]{1,0:T(8,128)(2,1)}), bf16[2048,256]{1,0:T(8,128)(2,1)}) %all-gather.5.cloned.1.call-update) | async-done | bytes 1048592 | tf_op jit(solution)/shard_map/all_gather | solution.py:51
  72.6 32.3 %gather_fusion.3 = bf16[8192,256]{1,0:T(8,128)(2,1)} fusion(bf16[2048,256]{1,0:T(8,128)(2,1)} %all-gather.5.cloned.1.call-done, s32[8192]{0:T(1024)S(1)} %broadcast_clamp_fusion), kind=kCustom, calls=%fused_computation.3 | custom fusion | bytes 8421376 | tf_op jit(solution)/shard_map/gather | solution.py:52
  104.9 51.3 %all-gather.3.cloned.1.call-done = bf16[8192,256]{1,0:T(8,128)(2,1)} async-done(((bf16[256,256]{1,0:T(8,128)(2,1)}), bf16[8192,256]{1,0:T(8,128)(2,1)}) %all-gather.3.cloned.1.call-update) | async-done | bytes 4194320 | tf_op jit(solution)/shard_map/all_gather | solution.py:48
  156.2 33.7 %gather_fusion.2 = bf16[8192,256]{1,0:T(8,128)(2,1)} fusion(bf16[8192,256]{1,0:T(8,128)(2,1)} %all-gather.3.cloned.1.call-done, s32[8192]{0:T(1024)S(1)} %broadcast_clamp_fusion.1), kind=kCustom, calls=%fused_computation.2 | custom fusion | bytes 8421376 | tf_op jit(solution)/shard_map/gather | solution.py:50
  189.9 3.6 fusion.16
  193.5 1.3 fusion
  194.7 2.4 fusion.6
  197.2 0.6 divide_subtract_fusion
  197.8 5.9 fusion.24
  203.7 2.0 copy-done.2
  205.7 4.5 fusion.1
  210.2 46.0 %scatter_custom_fusion.1 = f32[2048,256]{1,0:T(8,128)} fusion(s32[8192]{0:T(1024)S(1)} %bitcast.48, f32[8192,256]{1,0:T(8,128)} %fusion.1, f32[]{:T(128)} %constant.11.clone.1), kind=kCustom, calls=%fused_computation.25 | custom fusion | flops 2097152 | bytes 2097664 | tf_op jit(solution)/shard_map/scatter-add | solution.py:86
  256.2 0.0 reduce-scatter.5.cloned.1.call-update
  256.2 0.3 reduce-scatter.3.cloned.1.call-start
  256.5 6.7 fusion.2
  263.2 48.3 %scatter_custom_fusion = f32[8192,256]{1,0:T(8,128)} fusion(s32[8192]{0:T(1024)S(1)} %bitcast.46, f32[8192,256]{1,0:T(8,128)} %fusion.2, f32[]{:T(128)} %constant.11.clone.1), kind=kCustom, calls=%fused_computation.16 | custom fusion | flops 2097152 | bytes 8389120 | tf_op jit(solution)/shard_map/scatter-add | solution.py:80
  311.5 0.0 reduce-scatter.3.cloned.1.call-update
  311.5 0.0 copy-start.4
  311.5 0.0 all-reduce.6.cloned.1.call-start
  311.6 4.8 fusion.27
  316.4 0.0 reduce-scatter.5.cloned.1.call-done
  316.4 222.1 %reduce-scatter.3.cloned.1.call-done = f32[256,256]{1,0:T(8,128)} async-done(((f32[8192,256]{1,0:T(8,128)}), f32[256,256]{1,0:T(8,128)}) %reduce-scatter.3.cloned.1.call-update) | async-done | bytes 262160 | tf_op jit(solution)/shard_map/reduce_scatter | solution.py:82
  538.5 1.1 fusion.25
  539.6 0.9 fusion.18
  540.6 0.0 copy-done.4
  540.6 0.9 convolution_bitcast_fusion
  541.5 0.0 all-reduce.6.cloned.1.call-update
  541.5 0.0 copy-start.1
  541.5 0.0 all-reduce.8.cloned.1.call-start
  541.6 4.8 fusion.28
  546.4 0.8 maximum_bitcast_fusion
  547.2 141.1 %all-reduce.6.cloned.1.call-done = (f32[256,256]{0,1:T(8,128)}, f32[256,256]{1,0:T(8,128)}) async-done(((f32[256,256]{0,1:T(8,128)}, f32[256,256]{1,0:T(8,128)}), (f32[256,256]{0,1:T(8,128)}, f32[256,256]{1,0:T(8,128)})) %all-reduce.6.cloned.1.call-update) | async-done | bytes 524304 | tf_op jit(solution)/shard_map/psum | solution.py:94
  688.3 0.0 all-reduce.8.cloned.1.call-update
  688.3 62.9 %psum.67 = f32[256]{0:T(256)S(1)} all-reduce(f32[256]{0:T(256)S(1)} %get-tuple-element.46), channel_id=1, replica_groups=mesh['row'=8,'col'=32] {'col'}, use_global_device_ids=true, to_apply=%region_10.0 | all-reduce | flops 256 | bytes 2048 | tf_op jit(solution)/shard_map/psum | solution.py:94
  751.2 13.0 %all-reduce.1 = (f32[256]{0:T(256)}, f32[1,256]{1,0:T(1,128)}, f32[1,256]{1,0:T(1,128)}) all-reduce(f32[256]{0:T(256)S(1)} %psum.67, f32[1,256]{1,0:T(1,128)S(1)} %bitcast.52, f32[1,256]{1,0:T(1,128)S(1)} %bitcast.53), channel_id=1, replica_groups=mesh['row'=8,'col'=32] {'row'}, use_global_device_ids=true, to_apply=%region_11.0 | all-reduce | flops 768 | bytes 6144 | tf_op jit(solution)/shard_map/psum | solution.py:94
  764.1 1.8 copy.28
  765.9 1.7 copy.35
  767.6 1.9 copy.36
  (30 shorter events, 0.2 us)
Async XLA Ops:
  7.2 26.4 %copy-start = (bf16[256,256]{1,0:T(8,128)(2,1)S(1)}, bf16[256,256]{1,0:T(8,128)(2,1)}, u32[]{:S(2)}) copy-start(bf16[256,256]{1,0:T(8,128)(2,1)} %param.17) | copy-start | bytes 393220
  7.2 44.2 %copy-start.13 = (f32[256]{0:T(256)S(1)}, f32[256]{0:T(256)}, u32[]{:S(2)}) copy-start(f32[256]{0:T(256)} %param.19) | copy-start | bytes 3076
  7.2 44.2 %copy-start.7 = (bf16[256,256]{1,0:T(8,128)(2,1)S(1)}, bf16[256,256]{1,0:T(8,128)(2,1)}, u32[]{:S(2)}) copy-start(bf16[256,256]{1,0:T(8,128)(2,1)} %param.18) | copy-start | bytes 393220
  10.5 42.7 %copy-start.14 = (bf16[256]{0:T(256)(128)(2,1)S(1)}, bf16[256]{0:T(256)(128)(2,1)}, u32[]{:S(2)}) copy-start(bf16[256]{0:T(256)(128)(2,1)} %param.22) | copy-start | bytes 1540
  10.5 43.4 %copy-start.10 = (s32[1,1,8192]{2,1,0:T(1,128)S(1)}, s32[1,1,8192]{2,1,0:T(1,128)}, u32[]{:S(2)}) copy-start(s32[1,1,8192]{2,1,0:T(1,128)} %param.27) | copy-start | bytes 98308
  10.5 43.4 %copy-start.8 = (s32[1,1,8192]{2,1,0:T(1,128)S(1)}, s32[1,1,8192]{2,1,0:T(1,128)}, u32[]{:S(2)}) copy-start(s32[1,1,8192]{2,1,0:T(1,128)} %param.25) | copy-start | bytes 98308
  10.5 43.5 %copy-start.9 = (s32[1,1,8192,1]{2,3,1,0:T(1,128)S(1)}, s32[1,1,8192,1]{2,3,1,0:T(1,128)}, u32[]{:S(2)}) copy-start(s32[1,1,8192,1]{2,3,1,0:T(1,128)} %param.24) | copy-start | bytes 98308
  10.5 43.5 %copy-start.11 = (s32[1,1,8192]{2,1,0:T(1,128)S(1)}, s32[1,1,8192]{2,1,0:T(1,128)}, u32[]{:S(2)}) copy-start(s32[1,1,8192]{2,1,0:T(1,128)} %param.26) | copy-start | bytes 98308
  10.5 10.6 %all-to-all-start = ((bf16[1,8,32,256]{3,2,0,1:T(8,128)(2,1)}), bf16[1,8,32,256]{3,2,0,1:T(8,128)(2,1)S(1)}, u32[]{:S(2)}, u32[]{:S(2)}) async-start(bf16[1,8,32,256]{3,2,0,1:T(8,128)(2,1)} %bitcast.3), calls=%async_computation | async-start | bytes 262144 | tf_op jit(solution)/shard_map/all_to_all | solution.py:31
  21.8 20.8 %all-to-all-start.1 = ((bf16[1,8,32,256]{3,1,0,2:T(8,128)(2,1)}), bf16[1,8,32,256]{3,1,0,2:T(8,128)(2,1)S(1)}, u32[]{:S(2)}, u32[]{:S(2)}) async-start(bf16[1,8,32,256]{3,1,0,2:T(8,128)(2,1)} %copy.26), calls=%async_computation.1 | async-start | bytes 262144 | tf_op jit(solution)/shard_map/all_to_all | solution.py:30
  33.6 39.0 %all-gather.5.cloned.1.call-start = ((), (), s32[]{:S(2)}) async-start(), calls=%async_computation.5 | async-start | bytes 1179648 | tf_op jit(solution)/shard_map/all_gather | solution.py:51
  52.3 103.9 %all-gather.3.cloned.1.call-start = ((), (), s32[]{:S(2)}) async-start(), calls=%async_computation.4 | async-start | bytes 4325376 | tf_op jit(solution)/shard_map/all_gather | solution.py:48
  53.0 263.4 %reduce-scatter.5.cloned.1.call-start = ((), (), s32[]{:S(2)}) async-start(), calls=%async_computation.7 | async-start | bytes 2359296 | tf_op jit(solution)/shard_map/reduce_scatter | solution.py:88
  104.9 85.0 %copy-start.6 = (bf16[512,256]{1,0:T(8,128)(2,1)S(1)}, bf16[512,256]{1,0:T(8,128)(2,1)}, u32[]{:S(2)}) copy-start(bf16[512,256]{1,0:T(8,128)(2,1)} %param.20) | copy-start | bytes 786436
  189.9 3.6 copy-start.3
  189.9 3.6 copy-start.12
  203.7 2.0 copy-start.2
  256.2 282.3 %reduce-scatter.3.cloned.1.call-start = ((), (), s32[]{:S(2)}) async-start(), calls=%async_computation.6 | async-start | bytes 8650752 | tf_op jit(solution)/shard_map/reduce_scatter | solution.py:82
  311.5 229.0 %copy-start.4 = (bf16[256,256]{1,0:T(8,128)(2,1)S(1)}, bf16[256,256]{1,0:T(8,128)(2,1)}, u32[]{:S(2)}) copy-start(bf16[256,256]{1,0:T(8,128)(2,1)} %param.14) | copy-start | bytes 393220
  311.5 376.7 %all-reduce.6.cloned.1.call-start = ((), (), s32[]{:S(2)}) async-start(), calls=%async_computation.8 | async-start | bytes 1048576 | tf_op jit(solution)/shard_map/psum | solution.py:94
  539.6 6.7 copy-start.5
  541.5 227.9 %copy-start.1 = (bf16[256,256]{1,0:T(8,128)(2,1)S(1)}, bf16[256,256]{1,0:T(8,128)(2,1)}, u32[]{:S(2)}) copy-start(bf16[256,256]{1,0:T(8,128)(2,1)} %param.17) | copy-start | bytes 393220
  541.5 222.6 %all-reduce.8.cloned.1.call-start = ((), (), s32[]{:S(2)}) async-start(), calls=%async_computation.9 | async-start | bytes 2097152 | tf_op jit(solution)/shard_map/psum | solution.py:94
Sparse Core Ops, SparseCore 0:
  52.4 20.1 all-gather.4
  75.7 80.4 all-gather.2
  256.3 34.6 reduce-scatter.4
  311.6 226.8 reduce-scatter.2
  542.8 145.4 all-reduce.5
  691.2 65.9 all-reduce.7
